TPU v7x, 32 devices: a whole 2x2x4 slice. The times are simulated.
32 devices in a mesh: groups: 2 (over x), blk: 16 (over z, y, core).
Axes of the slice: x: 2, y: 2, z: 4, core: 2. Of those that a mesh axis runs over, the one named last changes fastest.
Arguments:
- hidden: bfloat16 [12288, 5120], P(('groups', 'blk')), parts along dimension 0, may hold values from -6 to 6
- norm_gain: float32 [5120], replicated, may hold values from 0.5 to 1.5
- q_weight: bfloat16 [5120, 2560], P('blk'), may hold values from -0.078125 to 0.078125
- q_bias: float32 [2560], replicated, may hold values from -5 to 5
- kv_store: bfloat16 [128, 2, 512, 512], P(('groups', 'blk')), parts along dimension 0, may hold values from -620 to 620
- block_home: int32 [128], P('groups'), parts along dimension 0, may hold values from 0 to 63, as said below
- need_ids: int32 [64, 2], P(('groups', 'blk')), parts along dimension 0, may hold values from 0 to 63, as said below
- hole_pos: int32 [64], P(('groups', 'blk')), parts along dimension 0, may hold values from 0 to 32767, as said below
- fill_len: int32 [64], P(('groups', 'blk')), parts along dimension 0, may hold values from 48 to 192
Outputs:
- attended: bfloat16 [12288, 2560], P(('groups', 'blk')), parts along dimension 0
There are 2 independent parts, one for each index of `groups`. A program takes and returns all parts, laid end to end along the dimension named above; an argument that names none is the same for every part. Nothing has to cross between parts.
Inputs may be any that keep to these rules, and one draw needn't show every extreme that they name: block_home is a permutation; block b is kept by device block_home[b] // 4 of blk. `need_ids`: the 4 blocks listed by the candidates of one device of blk are all different and are kept by different devices, each at most 2 places away from it along blk, counted around the loop. The span from hole_pos to hole_pos + fill_len - 1 lies inside the first block that the candidate lists.
All inputs are finite; a program needn't handle non-finite values.
Results may differ from a plain program's by a relative error of at most 0.0035.
The roundings to bfloat16 on the way count: a program that leaves them out, or rounds other values in their place, can miss the bound.
Values may be sent and summed in bfloat16 or wider, within the bound.
A program may use at most 128 MiB of HBM per device.

v0:
```python
import math

import jax
import jax.numpy as jnp
from jax import lax
from jax.sharding import PartitionSpec as P

HEAD_SIZE = 128
QUERY_HEADS = 20
KEY_HEADS = 4
BLOCK_TOKENS = 512
BLOCKS_NEEDED = 2
REACH = 2


def passed_along(block, axis, distance):
    devices = range(lax.axis_size(axis))
    route = [((i - distance) % len(devices), i) for i in devices]
    return lax.ppermute(block, axis, route)


def rms_normed(hidden, norm_gain):
    widened = hidden.astype(jnp.float32)
    scale_inv = lax.rsqrt(jnp.mean(widened * widened, axis=-1, keepdims=True) + 1e-06)
    return (widened * scale_inv * norm_gain).astype(jnp.bfloat16)


def attend_single(packed):
    candidate_query_rows, sketch_blocks, block_ids, hole_start, fill_rows = packed
    count_of_rows = candidate_query_rows.shape[0]
    block_key_rows = sketch_blocks[:, 0].reshape(BLOCKS_NEEDED * BLOCK_TOKENS, KEY_HEADS, HEAD_SIZE)
    block_value_rows = sketch_blocks[:, 1].reshape(
        BLOCKS_NEEDED * BLOCK_TOKENS, KEY_HEADS, HEAD_SIZE
    )
    query_matrix = candidate_query_rows.reshape(
        count_of_rows, KEY_HEADS, QUERY_HEADS // KEY_HEADS, HEAD_SIZE
    )
    scores = jnp.einsum(
        "rkgd,tkd->rkgt", query_matrix, block_key_rows, preferred_element_type=jnp.float32
    ) / math.sqrt(HEAD_SIZE)
    position = (
        block_ids[:, None] * BLOCK_TOKENS + jnp.arange(BLOCK_TOKENS, dtype=jnp.int32)[None, :]
    ).reshape(BLOCKS_NEEDED * BLOCK_TOKENS)
    masked = (position >= hole_start) & (position < hole_start + fill_rows)
    scores = jnp.where(masked[None, None, None, :], jnp.float32(-1e30), scores)
    row_max = jnp.max(scores, axis=-1, keepdims=True)
    exponent = jnp.exp(scores - row_max)
    denominator = jnp.sum(exponent, axis=-1)
    weights = exponent.astype(jnp.bfloat16)
    attended = (
        jnp.einsum("rkgt,tkd->rkgd", weights, block_value_rows, preferred_element_type=jnp.float32)
        / denominator[..., None]
    )
    attended = attended.reshape(count_of_rows, QUERY_HEADS * HEAD_SIZE)
    live_rows = jnp.arange(count_of_rows, dtype=jnp.int32) < fill_rows
    return jnp.where(live_rows[:, None], attended, jnp.float32(0.0)).astype(jnp.bfloat16)


def attend_all(query, sketch_blocks, block_lists, hole_starts, fill_rows):
    cand_count = block_lists.shape[0]
    count_of_rows = query.shape[0] // cand_count
    shaped = query.reshape(cand_count, count_of_rows, QUERY_HEADS * HEAD_SIZE)
    results = lax.map(attend_single, (shaped, sketch_blocks, block_lists, hole_starts, fill_rows))
    return results.reshape(cand_count * count_of_rows, QUERY_HEADS * HEAD_SIZE)


def shards(hidden, norm_gain, q_weight, q_bias, kv_store, block_home, need_ids, hole_pos, fill_len):
    normed = rms_normed(hidden, norm_gain)
    whole_weight = lax.all_gather(q_weight, "blk", axis=0, tiled=True)
    projected = jnp.dot(normed, whole_weight, preferred_element_type=jnp.float32)
    query = (projected + q_bias).astype(jnp.bfloat16)
    device_count = lax.axis_size("blk")
    myself = lax.axis_index("blk")
    local_count = kv_store.shape[0]
    empty_block = jnp.zeros(kv_store.shape[1:], kv_store.dtype)

    def select_block(block_lists):
        stored_at = block_home[block_lists.reshape(-1)]
        owned_here = stored_at // local_count == myself
        slot_index = jnp.sum(jnp.where(owned_here, stored_at % local_count, 0))
        has_block = jnp.any(owned_here)
        chosen = lax.dynamic_index_in_dim(kv_store, slot_index, 0, keepdims=False)
        return jnp.where(has_block, chosen, empty_block)

    incoming = []
    for offset in range(-REACH, REACH + 1):
        if offset == 0:
            incoming.append(select_block(need_ids))
        else:
            asked = passed_along(need_ids, "blk", -offset)
            incoming.append(passed_along(select_block(asked), "blk", offset))
    arrived = jnp.stack(incoming, axis=0)
    owners = block_home[need_ids] // local_count
    slot_of_entry = jnp.remainder(myself - owners + REACH, device_count)
    sketch_blocks = jnp.take(arrived, slot_of_entry, axis=0)
    return attend_all(query, sketch_blocks, need_ids, hole_pos, fill_len)


def solution(mesh):
    placed = (
        P(("groups", "blk"), None),
        P(),
        P("blk", None),
        P(),
        P(("groups", "blk"), None, None, None),
        P("groups"),
        P(("groups", "blk"), None),
        P(("groups", "blk")),
        P(("groups", "blk")),
    )
    return jax.shard_map(
        shards, mesh=mesh, in_specs=placed, out_specs=P(("groups", "blk"), None), check_vma=False
    )
```

profile of v0, /device:TPU:0, one launch (start us, length us, event | category | flops | bytes accessed | tf_op | source)
XLA Modules:
  0.0 285.8 jit_solution(10790405811085733742)
XLA Ops:
  7.8 2.6 collective-permute-start
  10.3 4.1 %collective-permute-start.4 = (s32[2,2]{1,0:T(2,128)}, s32[2,2]{1,0:T(2,128)S(1)}, u32[]{:S(2)}, u32[]{:S(2)}) collective-permute-start(s32[2,2]{1,0:T(2,128)} %param.17), channel_id=1, source_target_pairs={{1,0},{2,1},{3,2},{4,3},{5,4},{6,5},{7,6},{8,7},{9,8},{10,9},{11,1... | collective-permute-start | bytes 56 | tf_op jit(solution)/shard_map/ppermute | solution.py:19
  29.1 4.0 %select_bitcast_fusion.2 = (bf16[2,512,512]{2,1,0:T(8,128)(2,1)S(1)}, bf16[2,512,512]{2,1,0:T(8,128)(2,1)}) fusion(bf16[4,2,512,512]{3,2,1,0:T(8,128)(2,1)} %param.15, s32[]{:T(128)S(6)} %select_n.257, pred[]{:T(512)} %get-tuple-element.77, s32[]{:T(128)S(6)} %select_n.249, pred[]{:T(512)} %get-tuple-element.92), kind=kLoop, calls=%fused_computation.48 | loop fusion | flops 1048576 | bytes 4194314 | tf_op jit(solution)/shard_map/jit(_where)/select_n | solution.py:83
  33.1 2.8 collective-permute-start.1
  43.1 38.2 %collective-permute-done.1 = bf16[2,512,512]{2,1,0:T(8,128)(2,1)S(1)} collective-permute-done((bf16[2,512,512]{2,1,0:T(8,128)(2,1)}, bf16[2,512,512]{2,1,0:T(8,128)(2,1)S(1)}, u32[]{:S(2)}, u32[]{:S(2)}) %collective-permute-start.1) | collective-permute-done | bytes 1048608 | tf_op jit(solution)/shard_map/ppermute | solution.py:19
  81.3 33.3 %collective-permute-done.3 = bf16[2,512,512]{2,1,0:T(8,128)(2,1)S(1)} collective-permute-done((bf16[2,512,512]{2,1,0:T(8,128)(2,1)S(1)}, bf16[2,512,512]{2,1,0:T(8,128)(2,1)S(1)}, u32[]{:S(2)}, u32[]{:S(2)}) %collective-permute-start.3) | collective-permute-done | bytes 1048608 | tf_op jit(solution)/shard_map/ppermute | solution.py:19
  114.7 2.4 select_bitcast_fusion
  117.1 2.4 copy-done.4
  121.4 3.0 %fusion.15 = f32[384]{0:T(512)S(1)} fusion(bf16[384,5120]{1,0:T(8,128)(2,1)} %param.11), kind=kLoop, calls=%fused_computation.33 | loop fusion | flops 5897856 | bytes 3933696 | tf_op jit(solution)/shard_map/reduce_sum | solution.py:24
  124.4 45.0 %collective-permute-done.5 = bf16[2,512,512]{2,1,0:T(8,128)(2,1)S(1)} collective-permute-done((bf16[2,512,512]{2,1,0:T(8,128)(2,1)S(1)}, bf16[2,512,512]{2,1,0:T(8,128)(2,1)S(1)}, u32[]{:S(2)}, u32[]{:S(2)}) %collective-permute-start.5) | collective-permute-done | bytes 1048608 | tf_op jit(solution)/shard_map/ppermute | solution.py:19
  172.3 5.3 %gather_fusion.6 = bf16[4,2,512,512]{3,2,1,0:T(8,128)(2,1)} fusion(bf16[5,2,512,512]{3,2,1,0:T(8,128)(2,1)} %bitcast_dynamic-update-slice_fusion, s32[1024]{0:T(1024)S(1)} %pad_clamp_fusion), kind=kCustom, calls=%fused_computation.6 | custom fusion | bytes 8388624 | tf_op jit(solution)/shard_map/jit(_take)/gather | solution.py:95
  177.5 4.7 %broadcast_select_fusion = bf16[2,2,2,512,512]{4,3,2,1,0:T(8,128)(2,1)} fusion(bf16[2,2,2,512,512]{4,3,2,1,0:T(8,128)(2,1)} %bitcast.95, pred[2,2]{1,0:T(4,128)(4,1)S(1)} %compare_and_fusion.1), kind=kLoop, calls=%fused_computation.38 | loop fusion | flops 2097152 | bytes 8388612 | tf_op jit(solution)/shard_map/jit(_take)/select_n | solution.py:95
  182.3 30.0 %all-gather.2.cloned.1.call-done = bf16[5120,2560]{1,0:T(8,128)(2,1)} async-done(((bf16[320,2560]{1,0:T(8,128)(2,1)}), bf16[5120,2560]{1,0:T(8,128)(2,1)}) %all-gather.2.cloned.1.call-update) | async-done | bytes 26214416 | tf_op jit(solution)/shard_map/all_gather | solution.py:69
  212.3 17.5 %fusion.18 = bf16[384,2560]{1,0:T(8,128)(2,1)} fusion(bf16[5120,2560]{1,0:T(8,128)(2,1)} %all-gather.2.cloned.1.call-done, bf16[384,5120]{1,0:T(8,128)(2,1)} %param.11, f32[5120]{0:T(1024)S(1)} %copy-done.6, f32[384]{0:T(512)S(1)} %add_rsqrt_fusion, f32[2560]{0:T(1024)S(1)} %copy-done.7), kind=kOutput, calls=%fused_computation.37 | convolution fusion | flops 10076160000 | bytes 32144896 | tf_op jit(solution)/shard_map/dot_general | solution.py:70
  229.8 48.5 %while.10 = (s32[]{:T(128)}, bf16[2,192,2560]{2,1,0:T(8,128)(2,1)}, s32[2]{0:T(128)S(1)}, bf16[2,2,2,512,512]{4,3,2,1,0:T(8,128)(2,1)}, s32[2,2]{1,0:T(2,128)S(1...) while((s32[]{:T(128)}, bf16[2,192,2560]{2,1,0:T(8,128)(2,1)}, s32[2]{0:T(128)S(1)}, ...), condition=%wide.region_14.15_spmd, body=%wide.region_11.14_spmd.sunk | while | flops 2057990912 | bytes 79906376 | solution.py:63
  235.3 1.7 copy_bitcast_fusion.2
  238.3 1.3 squeeze.29
  240.8 2.9 %bitcast_reduce_fusion.2 = (f32[192,4,5]{0,2,1:T(8,128)S(1)}, f32[4,1024,192,5]{1,2,3,0:T(8,128)S(1)}) fusion(pred[1024]{0:T(1024)(128)(4,1)S(1)} %and.179, bf16[192,4,5,128]{0,3,2,1:T(8,128)(2,1)S(1)} %bitcast.91, bf16[1024,4,128,1]{2,1,0,3:T(4,128)(2,1)S(1)} %bitcast.93), kind=kOutput, calls=%fused_computation.8.clone.1 | convolution fusion | flops 1018425600 | bytes 17776640 | tf_op jit(solution)/shard_map/while/body/eval_jaxpr/rkgd,tkd->rkgt/dot_general | solution.py:38
  243.7 3.9 %fusion.48 = f32[192,4,5]{0,2,1:T(8,128)S(1)} fusion(f32[4,1024,192,5]{1,2,3,0:T(8,128)S(1)} %get-tuple-element.144, f32[192,4,5]{0,2,1:T(8,128)S(1)} %get-tuple-element.145, pred[1024]{0:T(1024)(128)(4,1)S(1)} %and.179), kind=kLoop, calls=%fused_computation.11.clone.1 | loop fusion | flops 15724800 | bytes 15760384 | tf_op jit(solution)/shard_map/while/body/eval_jaxpr/reduce_sum | solution.py:48
  247.7 3.9 %bitcast_divide_fusion.2 = bf16[192,4,5,128]{3,0,2,1:T(8,128)(2,1)S(1)} fusion(f32[4,1024,192,5]{1,2,3,0:T(8,128)S(1)} %get-tuple-element.144, f32[192,4,5]{0,2,1:T(8,128)S(1)} %get-tuple-element.145, pred[1024]{0:T(1024)(128)(4,1)S(1)} %and.179, bf16[1024,4,128,1]{2,1,0,3:T(4,128)(2,1)S(1)} %bitcast.94, f32[192,4,5]{0,2,1:T(8,128)S(1)} %fusion.48), kind=kOutput, calls=%fused_computation.17.clone.1 | convolution fusion | flops 1023344640 | bytes 17792000 | tf_op jit(solution)/shard_map/while/body/eval_jaxpr/rkgt,tkd->rkgd/dot_general | solution.py:51
  259.6 1.7 copy_bitcast_fusion.2
  265.0 2.9 %bitcast_reduce_fusion.2 = (f32[192,4,5]{0,2,1:T(8,128)S(1)}, f32[4,1024,192,5]{1,2,3,0:T(8,128)S(1)}) fusion(pred[1024]{0:T(1024)(128)(4,1)S(1)} %and.179, bf16[192,4,5,128]{0,3,2,1:T(8,128)(2,1)S(1)} %bitcast.91, bf16[1024,4,128,1]{2,1,0,3:T(4,128)(2,1)S(1)} %bitcast.93), kind=kOutput, calls=%fused_computation.8.clone.1 | convolution fusion | flops 1018425600 | bytes 17776640 | tf_op jit(solution)/shard_map/while/body/eval_jaxpr/rkgd,tkd->rkgt/dot_general | solution.py:38
  267.9 3.9 %fusion.48 = f32[192,4,5]{0,2,1:T(8,128)S(1)} fusion(f32[4,1024,192,5]{1,2,3,0:T(8,128)S(1)} %get-tuple-element.144, f32[192,4,5]{0,2,1:T(8,128)S(1)} %get-tuple-element.145, pred[1024]{0:T(1024)(128)(4,1)S(1)} %and.179), kind=kLoop, calls=%fused_computation.11.clone.1 | loop fusion | flops 15724800 | bytes 15760384 | tf_op jit(solution)/shard_map/while/body/eval_jaxpr/reduce_sum | solution.py:48
  271.9 3.9 %bitcast_divide_fusion.2 = bf16[192,4,5,128]{3,0,2,1:T(8,128)(2,1)S(1)} fusion(f32[4,1024,192,5]{1,2,3,0:T(8,128)S(1)} %get-tuple-element.144, f32[192,4,5]{0,2,1:T(8,128)S(1)} %get-tuple-element.145, pred[1024]{0:T(1024)(128)(4,1)S(1)} %and.179, bf16[1024,4,128,1]{2,1,0,3:T(4,128)(2,1)S(1)} %bitcast.94, f32[192,4,5]{0,2,1:T(8,128)S(1)} %fusion.48), kind=kOutput, calls=%fused_computation.17.clone.1 | convolution fusion | flops 1023344640 | bytes 17792000 | tf_op jit(solution)/shard_map/while/body/eval_jaxpr/rkgt,tkd->rkgd/dot_general | solution.py:51
  (105 shorter events, 38.4 us)
Async XLA Ops:
  6.5 10.1 %copy-start = (s32[64]{0:T(128)S(1)}, s32[64]{0:T(128)}, u32[]{:S(2)}) copy-start(s32[64]{0:T(128)} %param.16) | copy-start | bytes 772
  6.5 205.8 %all-gather.2.cloned.1.call-start = ((), (), s32[]{:S(2)}) async-start(), calls=%async_computation | async-start | bytes 27852800 | tf_op jit(solution)/shard_map/all_gather | solution.py:69
  7.3 14.2 %collective-permute-start.2 = (s32[2,2]{1,0:T(2,128)}, s32[2,2]{1,0:T(2,128)S(1)}, u32[]{:S(2)}, u32[]{:S(2)}) collective-permute-start(s32[2,2]{1,0:T(2,128)} %param.17), channel_id=1, source_target_pairs={{15,0},{0,1},{1,2},{2,3},{3,4},{4,5},{5,6},{6,7},{7,8},{8,9},{9,10... | collective-permute-start | bytes 56 | tf_op jit(solution)/shard_map/ppermute | solution.py:19
  7.8 14.5 %collective-permute-start = (s32[2,2]{1,0:T(2,128)}, s32[2,2]{1,0:T(2,128)S(1)}, u32[]{:S(2)}, u32[]{:S(2)}) collective-permute-start(s32[2,2]{1,0:T(2,128)} %param.17), channel_id=1, source_target_pairs={{14,0},{15,1},{0,2},{1,3},{2,4},{3,5},{4,6},{5,7},{6,8},{7,9},{8,1... | collective-permute-start | bytes 56 | tf_op jit(solution)/shard_map/ppermute | solution.py:19
  10.3 25.5 %collective-permute-start.4 = (s32[2,2]{1,0:T(2,128)}, s32[2,2]{1,0:T(2,128)S(1)}, u32[]{:S(2)}, u32[]{:S(2)}) collective-permute-start(s32[2,2]{1,0:T(2,128)} %param.17), channel_id=1, source_target_pairs={{1,0},{2,1},{3,2},{4,3},{5,4},{6,5},{7,6},{8,7},{9,8},{10,9},{11,1... | collective-permute-start | bytes 56 | tf_op jit(solution)/shard_map/ppermute | solution.py:19
  14.4 22.1 %collective-permute-start.6 = (s32[2,2]{1,0:T(2,128)}, s32[2,2]{1,0:T(2,128)S(1)}, u32[]{:S(2)}, u32[]{:S(2)}) collective-permute-start(s32[2,2]{1,0:T(2,128)} %param.17), channel_id=1, source_target_pairs={{2,0},{3,1},{4,2},{5,3},{6,4},{7,5},{8,6},{9,7},{10,8},{11,9},{12,... | collective-permute-start | bytes 56 | tf_op jit(solution)/shard_map/ppermute | solution.py:19
  33.1 48.2 %collective-permute-start.1 = (bf16[2,512,512]{2,1,0:T(8,128)(2,1)}, bf16[2,512,512]{2,1,0:T(8,128)(2,1)S(1)}, u32[]{:S(2)}, u32[]{:S(2)}) collective-permute-start(bf16[2,512,512]{2,1,0:T(8,128)(2,1)} %get-tuple-element.89), channel_id=1, source_target_pairs={{2,0},{3,1},{4,2},{5,3},{6,4},{7,5},{8,6},{9,7},{10,8},{11,9},{12,... | collective-permute-start | bytes 3145736 | tf_op jit(solution)/shard_map/ppermute | solution.py:19
  36.6 78.1 %collective-permute-start.3 = (bf16[2,512,512]{2,1,0:T(8,128)(2,1)S(1)}, bf16[2,512,512]{2,1,0:T(8,128)(2,1)S(1)}, u32[]{:S(2)}, u32[]{:S(2)}) collective-permute-start(bf16[2,512,512]{2,1,0:T(8,128)(2,1)S(1)} %get-tuple-element.88), channel_id=1, source_target_pairs={{1,0},{2,1},{3,2},{4,3},{5,4},{6,5},{7,6},{8,7},{9,8},{10,9},{11,1... | collective-permute-start | bytes 3145736 | tf_op jit(solution)/shard_map/ppermute | solution.py:19
  43.1 71.7 %copy-start.3 = (bf16[4,2,512,512]{3,2,1,0:T(8,128)(2,1)S(1)}, bf16[4,2,512,512]{3,2,1,0:T(8,128)(2,1)}, u32[]{:S(2)}) copy-start(bf16[4,2,512,512]{3,2,1,0:T(8,128)(2,1)} %param.15) | copy-start | bytes 12582916
  117.1 2.4 copy-start.4
  119.5 49.9 %collective-permute-start.5 = (bf16[2,512,512]{2,1,0:T(8,128)(2,1)S(1)}, bf16[2,512,512]{2,1,0:T(8,128)(2,1)S(1)}, u32[]{:S(2)}, u32[]{:S(2)}) collective-permute-start(bf16[2,512,512]{2,1,0:T(8,128)(2,1)S(1)} %get-tuple-element.87), channel_id=1, source_target_pairs={{15,0},{0,1},{1,2},{2,3},{3,4},{4,5},{5,6},{6,7},{7,8},{8,9},{9,10... | collective-permute-start | bytes 3145736 | tf_op jit(solution)/shard_map/ppermute | solution.py:19
  120.1 51.1 %collective-permute-start.7 = (bf16[2,512,512]{2,1,0:T(8,128)(2,1)S(1)}, bf16[2,512,512]{2,1,0:T(8,128)(2,1)S(1)}, u32[]{:S(2)}, u32[]{:S(2)}) collective-permute-start(bf16[2,512,512]{2,1,0:T(8,128)(2,1)S(1)} %get-tuple-element.85), channel_id=1, source_target_pairs={{14,0},{15,1},{0,2},{1,3},{2,4},{3,5},{4,6},{5,7},{6,8},{7,9},{8,1... | collective-permute-start | bytes 3145736 | tf_op jit(solution)/shard_map/ppermute | solution.py:19
  177.5 34.8 %copy-start.6 = (f32[5120]{0:T(1024)S(1)}, f32[5120]{0:T(1024)}, u32[]{:S(2)}) copy-start(f32[5120]{0:T(1024)} %param.12) | copy-start | bytes 61444
  177.5 34.8 %copy-start.7 = (f32[2560]{0:T(1024)S(1)}, f32[2560]{0:T(1024)}, u32[]{:S(2)}) copy-start(f32[2560]{0:T(1024)} %param.14) | copy-start | bytes 30724
  182.3 47.5 %copy-start.5 = (s32[2,2]{1,0:T(2,128)S(1)}, s32[2,2]{1,0:T(2,128)}, u32[]{:S(2)}) copy-start(s32[2,2]{1,0:T(2,128)} %param.17) | copy-start | bytes 52
  182.3 47.5 %copy-start.8 = (s32[2]{0:T(128)S(1)}, s32[2]{0:T(128)}, u32[]{:S(2)}) copy-start(s32[2]{0:T(128)} %param.19) | copy-start | bytes 28
  182.3 47.5 %copy-start.9 = (s32[2]{0:T(128)S(1)}, s32[2]{0:T(128)}, u32[]{:S(2)}) copy-start(s32[2]{0:T(128)} %param.18) | copy-start | bytes 28
  243.7 4.0 %copy-start.2 = (bf16[1024,4,128]{2,1,0:T(4,128)(2,1)S(1)}, bf16[1024,4,128]{2,1,0:T(4,128)(2,1)}, u32[]{:S(2)}) copy-start(bf16[1024,4,128]{2,1,0:T(4,128)(2,1)} %squeeze.30) | copy-start | bytes 3145732 | tf_op jit(solution)/shard_map/while
  267.9 4.0 %copy-start.2 = (bf16[1024,4,128]{2,1,0:T(4,128)(2,1)S(1)}, bf16[1024,4,128]{2,1,0:T(4,128)(2,1)}, u32[]{:S(2)}) copy-start(bf16[1024,4,128]{2,1,0:T(4,128)(2,1)} %squeeze.30) | copy-start | bytes 3145732 | tf_op jit(solution)/shard_map/while
  278.3 0.7 copy-start.1
Sparse Core Ops, SparseCore 0:
  9.0 203.3 all-gather.1
where the time goes:
time: 287 us; the launch traced here: 286 us
  waiting for transfers between devices  148 us (52%)
  local copies, waits for them, and re-layouts  37.2 us (13%)
  other arithmetic  31.4 us (11%)
  matrix products  31.2 us (11%)
  between operations  23.2 us (8%)
  starting transfers between devices  12.3 us (4%)
    ppermute x8, waiting for transfers between devices, passed_along(): return lax.ppermute(block, axis, route)  117 us
    all_gather x1, waiting for transfers between devices, shards(): whole_weight = lax.all_gather(q_weight, 'blk', axis=0, tiled=True)  30 us
    dot_general x1, matrix products, shards(): jnp.dot(normed, whole_weight, preferred_element_type=jnp.float32)  17.5 us
    ppermute x8, starting transfers between devices, passed_along(): return lax.ppermute(block, axis, route)  12.3 us
    reduce_sum x2, other arithmetic, attend_single(): denominator = jnp.sum(exponent, axis=-1)  7.9 us
    dot_general x2, matrix products, attend_single(): jnp.einsum('rkgt,tkd->rkgd', weights, block_value_rows, preferred_element...  7.83 us
    select_n x2, other arithmetic, select_block(): return jnp.where(has_block, chosen, empty_block)  6.33 us
    dynamic_slice x8, local copies, waits for them, and re-layouts, attend_all(): lax.map(attend_single, (shaped, sketch_blocks, block_lists, hole_starts,...  6.01 us
  transfers between devices with their start and end apart: 9, of which 5 were waited for; matrix products, arithmetic and copies ran while one was open for 12% of the time, Pallas kernels for 0%

commit v1 on v0

v1 whole, which is shorter than its diff:
```python
import math

import jax
import jax.numpy as jnp
from jax import lax
from jax.experimental import pallas as pl
from jax.experimental.pallas import tpu as pltpu
from jax.sharding import PartitionSpec as P

HEAD_SIZE = 128
QUERY_HEADS = 20
KEY_HEADS = 4
BLOCK_TOKENS = 512
BLOCKS_NEEDED = 2
REACH = 2


def passed_along(block, axis, distance):
    devices = range(lax.axis_size(axis))
    route = [((i - distance) % len(devices), i) for i in devices]
    return lax.ppermute(block, axis, route)


def rms_normed(hidden, norm_gain):
    widened = hidden.astype(jnp.float32)
    scale_inv = lax.rsqrt(jnp.mean(widened * widened, axis=-1, keepdims=True) + 1e-06)
    return (widened * scale_inv * norm_gain).astype(jnp.bfloat16)


def attend_kernel(slots, hole, fill, q_ref, first_ref, second_ref, out_ref):
    cand = pl.program_id(0)
    rows = q_ref.shape[0]
    factor = math.log2(math.e) / math.sqrt(HEAD_SIZE)
    live = fill[cand]
    start = hole[cand]
    column = lax.broadcasted_iota(jnp.int32, (rows, BLOCK_TOKENS), 1)
    masked = (column >= start) & (column < start + live)
    alive = lax.broadcasted_iota(jnp.int32, (rows, HEAD_SIZE), 0) < live
    over_keys = (((1,), (1,)), ((), ()))
    for head in range(QUERY_HEADS // KEY_HEADS):
        place = pl.ds(head * HEAD_SIZE, HEAD_SIZE)
        q = q_ref[:, place]
        near = lax.dot_general(q, first_ref[0, 0], over_keys, preferred_element_type=jnp.float32)
        far = lax.dot_general(q, second_ref[0, 0], over_keys, preferred_element_type=jnp.float32)
        near = jnp.where(masked, jnp.float32(-1e30), near)
        most = jnp.maximum(
            jnp.max(near, axis=-1, keepdims=True), jnp.max(far, axis=-1, keepdims=True)
        )
        near = jnp.exp2((near - most) * factor)
        far = jnp.exp2((far - most) * factor)
        total = jnp.sum(near, axis=-1, keepdims=True) + jnp.sum(far, axis=-1, keepdims=True)
        mixed = jnp.dot(
            near.astype(jnp.bfloat16), first_ref[0, 1], preferred_element_type=jnp.float32
        ) + jnp.dot(
            far.astype(jnp.bfloat16), second_ref[0, 1], preferred_element_type=jnp.float32
        )
        out_ref[:, place] = jnp.where(alive, mixed / total, 0.0).astype(jnp.bfloat16)


def attend(query, arrived, slots, need_ids, hole_pos, fill_len):
    cands = need_ids.shape[0]
    rows = query.shape[0] // cands
    width = QUERY_HEADS // KEY_HEADS * HEAD_SIZE
    hole = hole_pos - need_ids[:, 0] * BLOCK_TOKENS

    def sketch(entry):
        return pl.BlockSpec(
            (1, 2, BLOCK_TOKENS, HEAD_SIZE),
            lambda c, k, slots, hole, fill: (slots[c * BLOCKS_NEEDED + entry], 0, 0, k),
        )

    by_head = pl.BlockSpec((rows, width), lambda c, k, slots, hole, fill: (c, k))
    return pl.pallas_call(
        attend_kernel,
        grid_spec=pltpu.PrefetchScalarGridSpec(
            num_scalar_prefetch=3,
            grid=(cands, KEY_HEADS),
            in_specs=[by_head, sketch(0), sketch(1)],
            out_specs=by_head,
        ),
        out_shape=jax.ShapeDtypeStruct(query.shape, jnp.bfloat16),
        compiler_params=pltpu.CompilerParams(vmem_limit_bytes=40 * 1024 * 1024),
    )(slots.reshape(-1), hole, fill_len, query, arrived, arrived)


def shards(hidden, norm_gain, q_weight, q_bias, kv_store, block_home, need_ids, hole_pos, fill_len):
    normed = rms_normed(hidden, norm_gain)
    whole_weight = lax.all_gather(q_weight, "blk", axis=0, tiled=True)
    projected = jnp.dot(normed, whole_weight, preferred_element_type=jnp.float32)
    query = (projected + q_bias).astype(jnp.bfloat16)
    device_count = lax.axis_size("blk")
    myself = lax.axis_index("blk")
    local_count = kv_store.shape[0]
    empty_block = jnp.zeros(kv_store.shape[1:], kv_store.dtype)

    def select_block(block_lists):
        stored_at = block_home[block_lists.reshape(-1)]
        owned_here = stored_at // local_count == myself
        slot_index = jnp.sum(jnp.where(owned_here, stored_at % local_count, 0))
        has_block = jnp.any(owned_here)
        chosen = lax.dynamic_index_in_dim(kv_store, slot_index, 0, keepdims=False)
        return jnp.where(has_block, chosen, empty_block)

    incoming = []
    for offset in range(-REACH, REACH + 1):
        if offset == 0:
            incoming.append(select_block(need_ids))
        else:
            asked = passed_along(need_ids, "blk", -offset)
            incoming.append(passed_along(select_block(asked), "blk", offset))
    arrived = jnp.stack(incoming, axis=0)
    owners = block_home[need_ids] // local_count
    slot_of_entry = jnp.remainder(myself - owners + REACH, device_count)
    return attend(query, arrived, slot_of_entry, need_ids, hole_pos, fill_len)


def solution(mesh):
    placed = (
        P(("groups", "blk"), None),
        P(),
        P("blk", None),
        P(),
        P(("groups", "blk"), None, None, None),
        P("groups"),
        P(("groups", "blk"), None),
        P(("groups", "blk")),
        P(("groups", "blk")),
    )
    return jax.shard_map(
        shards, mesh=mesh, in_specs=placed, out_specs=P(("groups", "blk"), None), check_vma=False
    )
```

time: 287 us -> 257 us (0.90)
  local copies, waits for them, and re-layouts: 37.2 us -> 9.3 us
  Pallas kernels: 0 us -> 20.5 us
  matrix products: 31.2 us -> 16.6 us
  other arithmetic: 31.4 us -> 17.3 us
  waiting for transfers between devices: 148 us -> 157 us
    pallas_call x0 -> x1, Pallas kernels: none -> 20.5 us  [attend(): pl.pallas_call(attend_kernel, grid_spec=pltpu.PrefetchScalarGridSpec(num_...]
    dot_general x4 -> x0, matrix products: 13.7 us -> none  [the longest x2 7.83 us: attend_single(): jnp.einsum('rkgt,tkd->rkgd', weights, block_value_rows, preferred_element...]
    all_gather x1, waiting for transfers between devices: 30 us -> 40.5 us  [shards(): whole_weight = lax.all_gather(q_weight, 'blk', axis=0, tiled=True)]
    squeeze x6 -> x0, local copies, waits for them, and re-layouts: 8.41 us -> none  [the longest x2 3.47 us: attend_all(): lax.map(attend_single, (shaped, sketch_blocks, block_lists, hole_starts,...]
    reduce_sum x2 -> x0, other arithmetic: 7.9 us -> none  [attend_single(): denominator = jnp.sum(exponent, axis=-1)]
    dynamic_slice x8 -> x0, local copies, waits for them, and re-layouts: 6.01 us -> none  [attend_all(): lax.map(attend_single, (shaped, sketch_blocks, block_lists, hole_starts,...]
    gather x1 -> x0, local copies, waits for them, and re-layouts: 5.27 us -> none  [shards(): sketch_blocks = jnp.take(arrived, slot_of_entry, axis=0)]
    select_n x2 -> x1, other arithmetic: 4.76 us -> 0.02 us  [shards(): slot_of_entry = jnp.remainder(myself - owners + REACH, device_count)]
  transfers between devices with their start and end apart: 9 -> 9, of which waited for: 5 -> 5; matrix products, arithmetic and copies ran while one was open for 12% -> 10% of each run, Pallas kernels for 0% -> 0%
where the time goes in v1:
time: 257 us; the launch traced here: 256 us
  waiting for transfers between devices  157 us (61%)
  between operations  23.4 us (9%)
  Pallas kernels  20.5 us (8%)
  other arithmetic  17.3 us (7%)
  matrix products  16.6 us (6%)
  starting transfers between devices  12.1 us (5%)
  local copies, waits for them, and re-layouts  9.3 us (4%)
    ppermute x8, waiting for transfers between devices, passed_along(): return lax.ppermute(block, axis, route)  116 us
    all_gather x1, waiting for transfers between devices, shards(): whole_weight = lax.all_gather(q_weight, 'blk', axis=0, tiled=True)  40.5 us
    pallas_call x1, Pallas kernels, attend(): pl.pallas_call(attend_kernel, grid_spec=pltpu.PrefetchScalarGridSpec(num_...  20.5 us
    dot_general x1, matrix products, shards(): jnp.dot(normed, whole_weight, preferred_element_type=jnp.float32)  16.6 us
    ppermute x8, starting transfers between devices, passed_along(): return lax.ppermute(block, axis, route)  12.1 us
    select_n x2, other arithmetic, select_block(): return jnp.where(has_block, chosen, empty_block)  7.77 us
  transfers between devices with their start and end apart: 9, of which 5 were waited for; matrix products, arithmetic and copies ran while one was open for 10% of the time, Pallas kernels for 0%

profile of v1, /device:TPU:0, one launch (start us, length us, event | category | flops | bytes accessed | tf_op | source)
XLA Modules:
  0.0 256.3 jit_solution(1592033858819971880)
XLA Ops:
  7.3 3.0 %collective-permute-start = (s32[2,2]{1,0:T(2,128)}, s32[2,2]{1,0:T(2,128)S(1)}, u32[]{:S(2)}, u32[]{:S(2)}) collective-permute-start(s32[2,2]{1,0:T(2,128)} %param.15), channel_id=1, source_target_pairs={{14,0},{15,1},{0,2},{1,3},{2,4},{3,5},{4,6},{5,7},{6,8},{7,9},{8,1... | collective-permute-start | bytes 56 | tf_op jit(solution)/shard_map/ppermute | solution.py:21
  10.3 3.2 %collective-permute-start.6 = (s32[2,2]{1,0:T(2,128)}, s32[2,2]{1,0:T(2,128)S(1)}, u32[]{:S(2)}, u32[]{:S(2)}) collective-permute-start(s32[2,2]{1,0:T(2,128)} %param.15), channel_id=1, source_target_pairs={{2,0},{3,1},{4,2},{5,3},{6,4},{7,5},{8,6},{9,7},{10,8},{11,9},{12,... | collective-permute-start | bytes 56 | tf_op jit(solution)/shard_map/ppermute | solution.py:21
  13.5 1.4 collective-permute-start.4
  14.9 0.8 reshape.183
  17.1 0.7 compare_reduce_fusion.2
  21.9 0.7 compare_reduce_fusion.3
  28.0 4.1 %select_bitcast_fusion.2 = (bf16[2,512,512]{2,1,0:T(8,128)(2,1)S(1)}, bf16[2,512,512]{2,1,0:T(8,128)(2,1)}) fusion(bf16[4,2,512,512]{3,2,1,0:T(8,128)(2,1)} %param.13, s32[]{:T(128)S(6)} %select_n.199, pred[]{:T(512)} %get-tuple-element.11, s32[]{:T(128)S(6)} %select_n.191, pred[]{:T(512)} %get-tuple-element.22), kind=kLoop, calls=%fused_computation.22 | loop fusion | flops 1048576 | bytes 4194314 | tf_op jit(solution)/shard_map/jit(_where)/select_n | solution.py:102
  32.1 2.7 %collective-permute-start.1 = (bf16[2,512,512]{2,1,0:T(8,128)(2,1)}, bf16[2,512,512]{2,1,0:T(8,128)(2,1)S(1)}, u32[]{:S(2)}, u32[]{:S(2)}) collective-permute-start(bf16[2,512,512]{2,1,0:T(8,128)(2,1)} %get-tuple-element.19), channel_id=1, source_target_pairs={{2,0},{3,1},{4,2},{5,3},{6,4},{7,5},{8,6},{9,7},{10,8},{11,9},{12,... | collective-permute-start | bytes 3145736 | tf_op jit(solution)/shard_map/ppermute | solution.py:21
  36.3 0.7 compare_reduce_fusion
  39.0 0.7 fusion.17
  42.4 38.1 %collective-permute-done.1 = bf16[2,512,512]{2,1,0:T(8,128)(2,1)S(1)} collective-permute-done((bf16[2,512,512]{2,1,0:T(8,128)(2,1)}, bf16[2,512,512]{2,1,0:T(8,128)(2,1)S(1)}, u32[]{:S(2)}, u32[]{:S(2)}) %collective-permute-start.1) | collective-permute-done | bytes 1048608 | tf_op jit(solution)/shard_map/ppermute | solution.py:21
  80.5 1.0 bitcast_dynamic-update-slice_fusion.3
  81.5 32.2 %collective-permute-done.3 = bf16[2,512,512]{2,1,0:T(8,128)(2,1)S(1)} collective-permute-done((bf16[2,512,512]{2,1,0:T(8,128)(2,1)S(1)}, bf16[2,512,512]{2,1,0:T(8,128)(2,1)S(1)}, u32[]{:S(2)}, u32[]{:S(2)}) %collective-permute-start.3) | collective-permute-done | bytes 1048608 | tf_op jit(solution)/shard_map/ppermute | solution.py:21
  113.8 1.0 bitcast_dynamic-update-slice_fusion.2
  114.8 3.6 %select_bitcast_fusion = (bf16[2,512,512]{2,1,0:T(8,128)(2,1)S(1)}, bf16[5,2,512,512]{3,2,1,0:T(8,128)(2,1)}, bf16[2,512,512]{2,1,0:T(8,128)(2,1)S(1)}) fusion(bf16[4,2,512,512]{3,2,1,0:T(8,128)(2,1)S(1)} %copy-done.2, s32[]{:T(128)S(6)} %select_n.222, pred[]{:T(512)} %get-tuple-element.5, bf16[5,2,512,512]{3,2,1,0:T(8,128)(2,1)} %bitcast_dynamic-update-slice_fusion.2, ...), kind=kLoop, calls=%fused_computation.19 | loop fusion | flops 1572864 | bytes 6293004 | tf_op jit(solution)/shard_map/jit(_where)/select_n | solution.py:102
  119.9 1.2 collective-permute-start.7
  121.1 3.0 %fusion = f32[384]{0:T(512)S(1)} fusion(bf16[384,5120]{1,0:T(8,128)(2,1)} %param.9), kind=kLoop, calls=%fused_computation.8 | loop fusion | flops 5897856 | bytes 3933696 | tf_op jit(solution)/shard_map/reduce_sum | solution.py:26
  124.1 43.9 %collective-permute-done.5 = bf16[2,512,512]{2,1,0:T(8,128)(2,1)S(1)} collective-permute-done((bf16[2,512,512]{2,1,0:T(8,128)(2,1)S(1)}, bf16[2,512,512]{2,1,0:T(8,128)(2,1)S(1)}, u32[]{:S(2)}, u32[]{:S(2)}) %collective-permute-start.5) | collective-permute-done | bytes 1048608 | tf_op jit(solution)/shard_map/ppermute | solution.py:21
  168.0 1.1 bitcast_dynamic-update-slice_fusion.1
  169.1 1.7 collective-permute-done.7
  170.8 1.0 bitcast_dynamic-update-slice_fusion.first_ref.second_ref
  171.8 40.5 %all-gather.2.cloned.1.call-done = bf16[5120,2560]{1,0:T(8,128)(2,1)} async-done(((bf16[320,2560]{1,0:T(8,128)(2,1)}), bf16[5120,2560]{1,0:T(8,128)(2,1)}) %all-gather.2.cloned.1.call-update) | async-done | bytes 26214416 | tf_op jit(solution)/shard_map/all_gather | solution.py:88
  212.3 16.6 %fusion.3.q_ref = bf16[384,2560]{1,0:T(8,128)(2,1)S(1)} fusion(bf16[5120,2560]{1,0:T(8,128)(2,1)} %all-gather.2.cloned.1.call-done, bf16[384,5120]{1,0:T(8,128)(2,1)} %param.9, f32[5120]{0:T(1024)S(1)} %copy-done.4, f32[384]{0:T(512)S(1)} %add_rsqrt_fusion, f32[2560]{0:T(1024)S(1)} %copy-done.5), kind=kOutput, calls=%fused_computation.12 | convolution fusion | flops 10076160000 | bytes 32144896 | tf_op jit(solution)/shard_map/dot_general | solution.py:89
  228.9 20.5 %shard_map.91 = bf16[384,2560]{1,0:T(8,128)(2,1)} custom-call(s32[4]{0:T(128)S(1)} %and_select_fusion.10.slots, s32[2]{0:T(128)S(1)} %sub.33.hole, s32[2]{0:T(128)S(1)} %copy-done.1, bf16[384,2560]{1,0:T(8,128)(2,1)S(1)} %fusion.3.q_ref, bf16[5,2,512,512]{3,2,1,0:T(8,128)(2,1)} %bitcast_dynamic-update-slice_fusion.first_ref.second_ref, ...), custom_call_target="tpu_custom_call" | custom-call | tf_op jit(solution)/shard_map/pallas_call | solution.py:73
  (53 shorter events, 9.2 us)
Async XLA Ops:
  6.5 9.9 %copy-start = (s32[64]{0:T(128)S(1)}, s32[64]{0:T(128)}, u32[]{:S(2)}) copy-start(s32[64]{0:T(128)} %param.14) | copy-start | bytes 772
  6.5 205.8 %all-gather.2.cloned.1.call-start = ((), (), s32[]{:S(2)}) async-start(), calls=%async_computation | async-start | bytes 27852800 | tf_op jit(solution)/shard_map/all_gather | solution.py:88
  7.3 13.1 %collective-permute-start = (s32[2,2]{1,0:T(2,128)}, s32[2,2]{1,0:T(2,128)S(1)}, u32[]{:S(2)}, u32[]{:S(2)}) collective-permute-start(s32[2,2]{1,0:T(2,128)} %param.15), channel_id=1, source_target_pairs={{14,0},{15,1},{0,2},{1,3},{2,4},{3,5},{4,6},{5,7},{6,8},{7,9},{8,1... | collective-permute-start | bytes 56 | tf_op jit(solution)/shard_map/ppermute | solution.py:21
  10.3 10.9 %collective-permute-start.2 = (s32[2,2]{1,0:T(2,128)}, s32[2,2]{1,0:T(2,128)S(1)}, u32[]{:S(2)}, u32[]{:S(2)}) collective-permute-start(s32[2,2]{1,0:T(2,128)} %param.15), channel_id=1, source_target_pairs={{15,0},{0,1},{1,2},{2,3},{3,4},{4,5},{5,6},{6,7},{7,8},{8,9},{9,10... | collective-permute-start | bytes 56 | tf_op jit(solution)/shard_map/ppermute | solution.py:21
  10.3 24.5 %collective-permute-start.6 = (s32[2,2]{1,0:T(2,128)}, s32[2,2]{1,0:T(2,128)S(1)}, u32[]{:S(2)}, u32[]{:S(2)}) collective-permute-start(s32[2,2]{1,0:T(2,128)} %param.15), channel_id=1, source_target_pairs={{2,0},{3,1},{4,2},{5,3},{6,4},{7,5},{8,6},{9,7},{10,8},{11,9},{12,... | collective-permute-start | bytes 56 | tf_op jit(solution)/shard_map/ppermute | solution.py:21
  13.5 22.1 %collective-permute-start.4 = (s32[2,2]{1,0:T(2,128)}, s32[2,2]{1,0:T(2,128)S(1)}, u32[]{:S(2)}, u32[]{:S(2)}) collective-permute-start(s32[2,2]{1,0:T(2,128)} %param.15), channel_id=1, source_target_pairs={{1,0},{2,1},{3,2},{4,3},{5,4},{6,5},{7,6},{8,7},{9,8},{10,9},{11,1... | collective-permute-start | bytes 56 | tf_op jit(solution)/shard_map/ppermute | solution.py:21
  32.1 48.4 %collective-permute-start.1 = (bf16[2,512,512]{2,1,0:T(8,128)(2,1)}, bf16[2,512,512]{2,1,0:T(8,128)(2,1)S(1)}, u32[]{:S(2)}, u32[]{:S(2)}) collective-permute-start(bf16[2,512,512]{2,1,0:T(8,128)(2,1)} %get-tuple-element.19), channel_id=1, source_target_pairs={{2,0},{3,1},{4,2},{5,3},{6,4},{7,5},{8,6},{9,7},{10,8},{11,9},{12,... | collective-permute-start | bytes 3145736 | tf_op jit(solution)/shard_map/ppermute | solution.py:21
  35.5 78.2 %collective-permute-start.3 = (bf16[2,512,512]{2,1,0:T(8,128)(2,1)S(1)}, bf16[2,512,512]{2,1,0:T(8,128)(2,1)S(1)}, u32[]{:S(2)}, u32[]{:S(2)}) collective-permute-start(bf16[2,512,512]{2,1,0:T(8,128)(2,1)S(1)} %get-tuple-element.18), channel_id=1, source_target_pairs={{1,0},{2,1},{3,2},{4,3},{5,4},{6,5},{7,6},{8,7},{9,8},{10,9},{11,1... | collective-permute-start | bytes 3145736 | tf_op jit(solution)/shard_map/ppermute | solution.py:21
  42.4 72.4 %copy-start.2 = (bf16[4,2,512,512]{3,2,1,0:T(8,128)(2,1)S(1)}, bf16[4,2,512,512]{3,2,1,0:T(8,128)(2,1)}, u32[]{:S(2)}) copy-start(bf16[4,2,512,512]{3,2,1,0:T(8,128)(2,1)} %param.13) | copy-start | bytes 12582916
  81.5 38.2 %copy-start.3 = (s32[2,2]{1,0:T(2,128)S(1)}, s32[2,2]{1,0:T(2,128)}, u32[]{:S(2)}) copy-start(s32[2,2]{1,0:T(2,128)} %param.15) | copy-start | bytes 52
  81.5 38.3 %copy-start.6 = (s32[2]{0:T(128)S(1)}, s32[2]{0:T(128)}, u32[]{:S(2)}) copy-start(s32[2]{0:T(128)} %param.16) | copy-start | bytes 28
  118.4 93.9 %copy-start.4 = (f32[5120]{0:T(1024)S(1)}, f32[5120]{0:T(1024)}, u32[]{:S(2)}) copy-start(f32[5120]{0:T(1024)} %param.10) | copy-start | bytes 61444
  118.4 93.9 %copy-start.5 = (f32[2560]{0:T(1024)S(1)}, f32[2560]{0:T(1024)}, u32[]{:S(2)}) copy-start(f32[2560]{0:T(1024)} %param.12) | copy-start | bytes 30724
  118.4 49.5 %collective-permute-start.5 = (bf16[2,512,512]{2,1,0:T(8,128)(2,1)S(1)}, bf16[2,512,512]{2,1,0:T(8,128)(2,1)S(1)}, u32[]{:S(2)}, u32[]{:S(2)}) collective-permute-start(bf16[2,512,512]{2,1,0:T(8,128)(2,1)S(1)} %get-tuple-element.17), channel_id=1, source_target_pairs={{15,0},{0,1},{1,2},{2,3},{3,4},{4,5},{5,6},{6,7},{7,8},{8,9},{9,10... | collective-permute-start | bytes 3145736 | tf_op jit(solution)/shard_map/ppermute | solution.py:21
  119.9 50.9 %collective-permute-start.7 = (bf16[2,512,512]{2,1,0:T(8,128)(2,1)S(1)}, bf16[2,512,512]{2,1,0:T(8,128)(2,1)S(1)}, u32[]{:S(2)}, u32[]{:S(2)}) collective-permute-start(bf16[2,512,512]{2,1,0:T(8,128)(2,1)S(1)} %get-tuple-element.15), channel_id=1, source_target_pairs={{14,0},{15,1},{0,2},{1,3},{2,4},{3,5},{4,6},{5,7},{6,8},{7,9},{8,1... | collective-permute-start | bytes 3145736 | tf_op jit(solution)/shard_map/ppermute | solution.py:21
  171.8 57.1 %copy-start.1 = (s32[2]{0:T(128)S(1)}, s32[2]{0:T(128)}, u32[]{:S(2)}) copy-start(s32[2]{0:T(128)} %fill.1) | copy-start | bytes 28
Sparse Core Ops, SparseCore 0:
  9.0 203.3 all-gather.1

commit v2 on v1

--- a/solution.py
+++ b/solution.py
@@ -1,3 +1,4 @@
+import functools
 import math
 
 import jax
@@ -13,18 +14,263 @@
 BLOCK_TOKENS = 512
 BLOCKS_NEEDED = 2
 REACH = 2
-
-
-def passed_along(block, axis, distance):
-    devices = range(lax.axis_size(axis))
-    route = [((i - distance) % len(devices), i) for i in devices]
-    return lax.ppermute(block, axis, route)
-
-
-def rms_normed(hidden, norm_gain):
-    widened = hidden.astype(jnp.float32)
-    scale_inv = lax.rsqrt(jnp.mean(widened * widened, axis=-1, keepdims=True) + 1e-06)
-    return (widened * scale_inv * norm_gain).astype(jnp.bfloat16)
+MESH = pl.DeviceIdType.MESH
+
+
+def exchange_kernel(ids_ref, out_ref, send_sem, recv_sem):
+    count = lax.axis_size("blk")
+    me = lax.axis_index("blk")
+    barrier = pltpu.get_barrier_semaphore()
+    offsets = [o for o in range(-REACH, REACH + 1) if o]
+    for o in offsets:
+        pl.semaphore_signal(
+            barrier, inc=1, device_id={"blk": lax.rem(me + o + count, count)}, device_id_type=MESH
+        )
+    pl.semaphore_wait(barrier, len(offsets))
+    copies = []
+    for o in offsets:
+        copy = pltpu.make_async_remote_copy(
+            src_ref=ids_ref,
+            dst_ref=out_ref.at[o + REACH],
+            send_sem=send_sem.at[o + REACH],
+            recv_sem=recv_sem.at[o + REACH],
+            device_id={"blk": lax.rem(me - o + count, count)},
+            device_id_type=MESH,
+        )
+        copy.start()
+        copies.append(copy)
+    out_ref[REACH] = ids_ref[...]
+    for copy in copies:
+        copy.wait()
+
+
+def exchanged(need_ids):
+    cands, needed = need_ids.shape
+    padded = jnp.pad(need_ids, ((0, 8 - cands), (0, 128 - needed)))
+    span = 2 * REACH + 1
+    out = pl.pallas_call(
+        exchange_kernel,
+        out_shape=jax.ShapeDtypeStruct((span, 8, 128), jnp.int32),
+        in_specs=[pl.BlockSpec(memory_space=pltpu.VMEM)],
+        out_specs=pl.BlockSpec(memory_space=pltpu.VMEM),
+        scratch_shapes=[pltpu.SemaphoreType.DMA((span,)), pltpu.SemaphoreType.DMA((span,))],
+        compiler_params=pltpu.CompilerParams(collective_id=0, has_side_effects=True),
+    )(padded)
+    return out[:, :cands, :needed].reshape(span, cands * needed)
+
+
+def pick_kernel(slots, in_ref, out_ref):
+    out_ref[...] = in_ref[...]
+
+
+def picked_blocks(slots, kv_store):
+    block = (1,) + kv_store.shape[1:]
+    return pl.pallas_call(
+        pick_kernel,
+        grid_spec=pltpu.PrefetchScalarGridSpec(
+            num_scalar_prefetch=1,
+            grid=slots.shape,
+            in_specs=[pl.BlockSpec(block, lambda i, slots: (slots[i], 0, 0, 0))],
+            out_specs=pl.BlockSpec(block, lambda i, slots: (i, 0, 0, 0)),
+        ),
+        out_shape=jax.ShapeDtypeStruct(slots.shape + kv_store.shape[1:], kv_store.dtype),
+        compiler_params=pltpu.CompilerParams(vmem_limit_bytes=16 * 1024 * 1024),
+    )(slots, kv_store)
+
+
+def project_kernel(
+    chips, snake, hidden, gain, weight, bias, picked, query, arrived,
+    whole, normed, acc, recv, to_ahead, to_behind, to_sibling, to_partner, kv_send, kv_recv, kv_own,
+):
+    group, me = lax.axis_index("groups"), lax.axis_index("blk")
+    count = 2 * chips
+    half = chips // 2
+    place, core, side = lax.div(me, 2), lax.rem(me, 2), lax.rem(group, 2)
+    depth, width = weight.shape[0], weight.shape[1] // 2
+
+    def ring_of(chip):
+        if not snake:
+            return chip
+        z, y = lax.div(chip, 2), lax.rem(chip, 2)
+        return z + y * (chips - 1 - 2 * z)
+
+    def chip_of(spot):
+        spot = lax.rem(spot + chips, chips)
+        if not snake:
+            return spot
+        y = lax.div(spot, half)
+        return (spot + y * (chips - 1 - 2 * spot)) * 2 + y
+
+    spot = ring_of(place)
+    turn = 1 - 2 * core
+    ahead = {"blk": chip_of(spot + turn) * 2 + core}
+    behind = {"blk": chip_of(spot - turn) * 2 + core}
+    sibling = {"blk": me + turn}
+    partner = {"groups": group + 1 - 2 * side}
+    offsets = [o for o in (1, -1, 2, -2)]
+
+    def near(o):
+        return {"blk": lax.rem(me + o + count, count)}
+
+    greeted = [ahead, behind, sibling, partner] + [near(o) for o in offsets]
+    barrier = pltpu.get_barrier_semaphore()
+    for other in greeted:
+        pl.semaphore_signal(barrier, inc=1, device_id=other, device_id_type=MESH)
+    for h in range(2):
+        whole[place, h, core] = weight[:, h * width : (h + 1) * width]
+    pl.semaphore_wait(barrier, len(greeted))
+
+    sent = []
+
+    def piece(origin, h, c, sem, other):
+        return pltpu.make_async_remote_copy(
+            src_ref=whole.at[origin, h, c],
+            dst_ref=whole.at[origin, h, c],
+            send_sem=sem,
+            recv_sem=recv.at[origin, h, c],
+            device_id=other,
+            device_id_type=MESH,
+        )
+
+    def send(origin, h, sem, other):
+        copy = piece(origin, h, core, sem, other)
+        copy.start()
+        sent.append(copy)
+
+    def landed(origin, h, c):
+        piece(origin, h, c, to_sibling.at[origin, h], sibling).wait_recv()
+
+    send(place, side, to_ahead.at[place], ahead)
+    send(place, side, to_behind.at[place], behind)
+    for h in range(2):
+        send(place, h, to_sibling.at[place, h], sibling)
+    kv_copies = []
+    for o in offsets:
+        copy = pltpu.make_async_remote_copy(
+            src_ref=picked.at[o + REACH],
+            dst_ref=arrived.at[o + REACH],
+            send_sem=kv_send.at[o + REACH],
+            recv_sem=kv_recv.at[o + REACH],
+            device_id=near(o),
+            device_id_type=MESH,
+        )
+        copy.start()
+        kv_copies.append(copy)
+    own = pltpu.make_async_copy(picked.at[REACH], arrived.at[REACH], kv_own)
+    own.start()
+
+    tile = 32
+    part = normed.shape[2]
+
+    @pl.loop(0, hidden.shape[0] // tile)
+    def _(i):
+        rows = pl.ds(pl.multiple_of(i * tile, tile), tile)
+        widened = hidden[rows, :].astype(jnp.float32)
+        scale_inv = lax.rsqrt(jnp.mean(widened * widened, axis=-1, keepdims=True) + 1e-06)
+        scaled = (widened * scale_inv * gain[...]).astype(jnp.bfloat16)
+        for chip in range(chips):
+            normed[chip, rows, :] = scaled[:, chip * part : (chip + 1) * part]
+
+    columns = 256
+
+    def multiply(origin, first):
+        for h in range(2):
+            landed(origin, h, 1 - core)
+
+        @pl.loop(0, 2 * (width // columns))
+        def _(i):
+            h = lax.div(i, width // columns)
+            t = lax.rem(i, width // columns)
+            cols = pl.ds(pl.multiple_of(t * columns, columns), columns)
+            block = whole[origin, h, :, :, cols].reshape(2 * depth, columns)
+            product = jnp.dot(normed[origin], block, preferred_element_type=jnp.float32)
+            if first:
+                acc[h, :, cols] = product
+            else:
+                acc[h, :, cols] += product
+
+    def origins(k):
+        return [chip_of(spot - turn * k)] + ([chip_of(spot + turn * k)] if k < half else [])
+
+    def from_ring(k):
+        for origin, sem, other, last in zip(
+            origins(k), (to_ahead, to_behind), (ahead, behind), (half, half - 1)
+        ):
+            landed(origin, side, core)
+            if k < last:
+                send(origin, side, sem.at[origin], other)
+            send(origin, side, to_partner.at[origin], partner)
+            send(origin, side, to_sibling.at[origin, side], sibling)
+
+    def from_partner(k):
+        for origin in origins(k):
+            landed(origin, 1 - side, core)
+            send(origin, 1 - side, to_sibling.at[origin, 1 - side], sibling)
+
+    def multiply_step(k):
+        for origin in origins(k):
+            multiply(origin, False)
+
+    multiply(place, True)
+    for k in range(1, half + 4):
+        if k <= half:
+            from_ring(k)
+        if 1 <= k - 2 <= half:
+            from_partner(k - 2)
+        if 1 <= k - 3 <= half:
+            multiply_step(k - 3)
+
+    for h in range(2):
+        for t in range(width // columns):
+            lane = h * width + t * columns
+            query[:, lane : lane + columns] = (
+                acc[h, :, t * columns : (t + 1) * columns] + bias[:, lane : lane + columns]
+            ).astype(jnp.bfloat16)
+    for copy in sent:
+        copy.wait_send()
+    for copy in kv_copies:
+        copy.wait()
+    own.wait()
+
+
+def projected(hidden, norm_gain, q_weight, q_bias, picked):
+    rows, features = hidden.shape
+    depth, outputs = q_weight.shape
+    chips = lax.axis_size("blk") // 2
+    vmem = pl.BlockSpec(memory_space=pltpu.VMEM)
+    anywhere = pl.BlockSpec(memory_space=pl.ANY)
+    dma = pltpu.SemaphoreType.DMA
+    span = 2 * REACH + 1
+    return pl.pallas_call(
+        functools.partial(project_kernel, chips, lax.axis_size("groups") == 2),
+        out_shape=(
+            jax.ShapeDtypeStruct((rows, outputs), jnp.bfloat16),
+            jax.ShapeDtypeStruct(picked.shape, picked.dtype),
+        ),
+        in_specs=[vmem, vmem, vmem, vmem, anywhere],
+        out_specs=(vmem, anywhere),
+        scratch_shapes=[
+            pltpu.VMEM((chips, 2, 2, depth, outputs // 2), jnp.bfloat16),
+            pltpu.VMEM((chips, rows, features // chips), jnp.bfloat16),
+            pltpu.VMEM((2, rows, outputs // 2), jnp.float32),
+            dma((chips, 2, 2)),
+            dma((chips,)),
+            dma((chips,)),
+            dma((chips, 2)),
+            dma((chips,)),
+            dma((span,)),
+            dma((span,)),
+            dma,
+        ],
+        compiler_params=pltpu.CompilerParams(
+            collective_id=1, has_side_effects=True, vmem_limit_bytes=56 * 1024 * 1024
+        ),
+        cost_estimate=pl.CostEstimate(
+            flops=2 * rows * features * outputs,
+            bytes_accessed=2 * picked.size * 2 + rows * features * 2,
+            transcendentals=0,
+        ),
+    )(hidden, norm_gain.reshape(1, -1), q_weight, q_bias.reshape(1, -1), picked)
 
 
 def attend_kernel(slots, hole, fill, q_ref, first_ref, second_ref, out_ref):
@@ -84,31 +330,14 @@
 
 
 def shards(hidden, norm_gain, q_weight, q_bias, kv_store, block_home, need_ids, hole_pos, fill_len):
-    normed = rms_normed(hidden, norm_gain)
-    whole_weight = lax.all_gather(q_weight, "blk", axis=0, tiled=True)
-    projected = jnp.dot(normed, whole_weight, preferred_element_type=jnp.float32)
-    query = (projected + q_bias).astype(jnp.bfloat16)
     device_count = lax.axis_size("blk")
     myself = lax.axis_index("blk")
     local_count = kv_store.shape[0]
-    empty_block = jnp.zeros(kv_store.shape[1:], kv_store.dtype)
-
-    def select_block(block_lists):
-        stored_at = block_home[block_lists.reshape(-1)]
-        owned_here = stored_at // local_count == myself
-        slot_index = jnp.sum(jnp.where(owned_here, stored_at % local_count, 0))
-        has_block = jnp.any(owned_here)
-        chosen = lax.dynamic_index_in_dim(kv_store, slot_index, 0, keepdims=False)
-        return jnp.where(has_block, chosen, empty_block)
-
-    incoming = []
-    for offset in range(-REACH, REACH + 1):
-        if offset == 0:
-            incoming.append(select_block(need_ids))
-        else:
-            asked = passed_along(need_ids, "blk", -offset)
-            incoming.append(passed_along(select_block(asked), "blk", offset))
-    arrived = jnp.stack(incoming, axis=0)
+    stored_at = block_home[exchanged(need_ids)]
+    owned_here = stored_at // local_count == myself
+    slots = jnp.sum(jnp.where(owned_here, stored_at % local_count, 0), axis=1)
+    picked = picked_blocks(slots, kv_store)
+    query, arrived = projected(hidden, norm_gain, q_weight, q_bias, picked)
     owners = block_home[need_ids] // local_count
     slot_of_entry = jnp.remainder(myself - owners + REACH, device_count)
     return attend(query, arrived, slot_of_entry, need_ids, hole_pos, fill_len)

time: 257 us -> 237 us (0.922)
  Pallas kernels: 20.5 us -> 221 us
  waiting for transfers between devices: 157 us -> 0 us
  between operations: 23.4 us -> 0.1 us
  other arithmetic: 17.3 us -> 0.29 us
  matrix products: 16.6 us -> 0 us
  starting transfers between devices: 12.1 us -> 0 us
  local copies, waits for them, and re-layouts: 9.3 us -> 12.9 us
    pallas_call x0 -> x3, Pallas kernels: none -> 200 us  [the longest x1 190 us: projected(): pl.pallas_call(functools.partial(project_kernel, chips, lax.axis_size('gr...]
    ppermute x8 -> x0, waiting for transfers between devices: 116 us -> none  [passed_along(): return lax.ppermute(block, axis, route)]
    all_gather x1 -> x0, waiting for transfers between devices: 40.5 us -> none  [shards(): whole_weight = lax.all_gather(q_weight, 'blk', axis=0, tiled=True)]
    dot_general x1 -> x0, matrix products: 16.6 us -> none  [shards(): jnp.dot(normed, whole_weight, preferred_element_type=jnp.float32)]
    ppermute x8 -> x0, starting transfers between devices: 12.1 us -> none  [passed_along(): return lax.ppermute(block, axis, route)]
    select_n x7 -> x1, other arithmetic: 7.8 us -> 0.01 us  [shards(): stored_at = block_home[exchanged(need_ids)]]
    reduce_sum x6 -> x1, other arithmetic: 6.44 us -> 0.13 us  [shards(): slots = jnp.sum(jnp.where(owned_here, stored_at % local_count, 0), axis=1)]
    unnamed x17 -> x18, local copies, waits for them, and re-layouts: 3.22 us -> 8.52 us
  transfers between devices with their start and end apart: 9 -> 0, of which waited for: 5 -> 0; matrix products, arithmetic and copies ran while one was open for 10% -> 0% of each run, Pallas kernels for 0% -> 0%
where the time goes in v2:
time: 237 us; the launch traced here: 234 us
  Pallas kernels  221 us (93%)
  local copies, waits for them, and re-layouts  12.9 us (5%)
    pallas_call x1, Pallas kernels, projected(): pl.pallas_call(functools.partial(project_kernel, chips, lax.axis_size('gr...  190 us
    pallas_call x1, Pallas kernels, attend(): pl.pallas_call(attend_kernel, grid_spec=pltpu.PrefetchScalarGridSpec(num_...  20.2 us
    pallas_call x1, Pallas kernels, exchanged(): pl.pallas_call(exchange_kernel, out_shape=jax.ShapeDtypeStruct((span, 8,...  9.48 us
    unnamed x18, local copies, waits for them, and re-layouts  8.52 us

profile of v2, /device:TPU:0, one launch (start us, length us, event | category | flops | bytes accessed | tf_op | source)
XLA Modules:
  0.0 233.8 jit_solution(14183544248844434267)
XLA Ops:
  0.0 0.0 copy-start
  0.0 1.3 pad.4.ids_ref
  1.3 9.5 %shard_map.91 = s32[5,8,128]{2,1,0:T(8,128)} custom-call(s32[8,128]{1,0:T(8,128)} %pad.4.ids_ref), custom_call_target="tpu_custom_call" | custom-call | tf_op jit(solution)/shard_map/pallas_call | solution.py:51
  10.8 0.7 slice.7
  11.5 0.1 copy.12
  11.6 0.1 copy.13
  11.7 0.1 reshape.54
  11.8 0.0 copy-done
  11.8 0.7 gather_fusion.1
  12.5 0.1 reshape.53
  12.6 0.1 fusion.2.slots
  12.7 0.0 copy-start.3
  12.7 2.2 copy-done.3
  14.9 1.0 shard_map.92.picked
  15.9 0.0 copy-start.2
  15.9 2.3 copy-done.2
  18.2 0.6 reshape.42.bias
  18.8 189.9 %shard_map.93 = (bf16[384,2560]{1,0:T(8,128)(2,1)}, bf16[5,2,512,512]{3,2,1,0:T(8,128)(2,1)}) custom-call(bf16[384,5120]{1,0:T(8,128)(2,1)} %hidden.1, f32[1,5120]{1,0:T(1,128)} %bitcast.5, bf16[320,2560]{1,0:T(8,128)(2,1)} %weight.1, f32[1,2560]{1,0:T(1,128)} %reshape.42.bias, bf16[5,2,512,512]{3,2,1,0:T(8,128)(2,1)} %copy-done.2), custom_call_target="tpu_custom_call" | custom-call | flops 10066329600 | bytes 14417920 | tf_op jit(solution)/shard_map/pallas_call | solution.py:244
  208.7 0.1 reshape.46
  208.8 0.6 gather_fusion
  209.5 0.1 multiply_reduce_fusion
  209.6 2.5 %copy-done.1 = bf16[5,2,512,512]{3,2,1,0:T(8,128)(2,1)S(1)} copy-done((bf16[5,2,512,512]{3,2,1,0:T(8,128)(2,1)S(1)}, bf16[5,2,512,512]{3,2,1,0:T(8,128)(2,1)}, u32[]{:S(2)}) %copy-start.1) | copy-done | bytes 5242904
  212.1 1.5 copy-done.4
  213.6 20.2 %shard_map.94 = bf16[384,2560]{1,0:T(8,128)(2,1)} custom-call(s32[4]{0:T(128)S(1)} %and_select_fusion.slots, s32[2]{0:T(128)S(1)} %sub.21.hole, s32[2]{0:T(128)S(1)} %copy-done.5, bf16[384,2560]{1,0:T(8,128)(2,1)S(1)} %copy-done.4, bf16[5,2,512,512]{3,2,1,0:T(8,128)(2,1)S(1)} %copy-done.1, bf16[5,2,512,512]{3,2,1,0:T(8,128)(2,1)S(1)} %copy-done.1), custom_call_target="tpu_custom_call" | custom-call | tf_op jit(solution)/shard_map/pallas_call | solution.py:319
  (16 shorter events, 0.1 us)
Async XLA Ops:
  0.0 11.8 %copy-start = (s32[64]{0:T(128)S(1)}, s32[64]{0:T(128)}, u32[]{:S(2)}) copy-start(s32[64]{0:T(128)} %param.14) | copy-start | bytes 772
  12.7 2.2 copy-start.3
  14.9 3.3 %copy-start.6 = (f32[2560]{0:T(1024)S(1)}, f32[2560]{0:T(1024)}, u32[]{:S(2)}) copy-start(f32[2560]{0:T(1024)} %param.12) | copy-start | bytes 30724
  15.9 2.3 copy-start.2
  18.8 189.9 %copy-start.7 = (s32[2,2]{1,0:T(2,128)S(1)}, s32[2,2]{1,0:T(2,128)}, u32[]{:S(2)}) copy-start(s32[2,2]{1,0:T(2,128)} %param.15) | copy-start | bytes 52
  18.8 190.8 %copy-start.8 = (s32[2]{0:T(128)S(1)}, s32[2]{0:T(128)}, u32[]{:S(2)}) copy-start(s32[2]{0:T(128)} %param.16) | copy-start | bytes 28
  18.8 190.8 %copy-start.5 = (s32[2]{0:T(128)S(1)}, s32[2]{0:T(128)}, u32[]{:S(2)}) copy-start(s32[2]{0:T(128)} %fill.1) | copy-start | bytes 28
  209.6 2.5 %copy-start.1 = (bf16[5,2,512,512]{3,2,1,0:T(8,128)(2,1)S(1)}, bf16[5,2,512,512]{3,2,1,0:T(8,128)(2,1)}, u32[]{:S(2)}) copy-start(bf16[5,2,512,512]{3,2,1,0:T(8,128)(2,1)} %get-tuple-element.8.first_ref.second_ref) | copy-start | bytes 15728644
  212.1 1.5 copy-start.4

commit v3 on v2

--- a/solution.py
+++ b/solution.py
@@ -15,6 +15,8 @@
 BLOCKS_NEEDED = 2
 REACH = 2
 MESH = pl.DeviceIdType.MESH
+CHUNKS = 2
+KV_STEP = 4
 
 
 def exchange_kernel(ids_ref, out_ref, send_sem, recv_sem):
@@ -74,19 +76,20 @@
             out_specs=pl.BlockSpec(block, lambda i, slots: (i, 0, 0, 0)),
         ),
         out_shape=jax.ShapeDtypeStruct(slots.shape + kv_store.shape[1:], kv_store.dtype),
-        compiler_params=pltpu.CompilerParams(vmem_limit_bytes=16 * 1024 * 1024),
+        compiler_params=pltpu.CompilerParams(vmem_limit_bytes=58 * 1024 * 1024),
     )(slots, kv_store)
 
 
 def project_kernel(
-    chips, snake, hidden, gain, weight, bias, picked, query, arrived,
+    chips, snake, hidden_far, gain, weight, bias, picked, query, arrived,
     whole, normed, acc, recv, to_ahead, to_behind, to_sibling, to_partner, kv_send, kv_recv, kv_own,
+    hidden, hidden_sem,
 ):
     group, me = lax.axis_index("groups"), lax.axis_index("blk")
     count = 2 * chips
     half = chips // 2
     place, core, side = lax.div(me, 2), lax.rem(me, 2), lax.rem(group, 2)
-    depth, width = weight.shape[0], weight.shape[1] // 2
+    depth, width = weight.shape[0], weight.shape[1] // (2 * CHUNKS)
 
     def ring_of(chip):
         if not snake:
@@ -113,10 +116,12 @@
         return {"blk": lax.rem(me + o + count, count)}
 
     greeted = [ahead, behind, sibling, partner] + [near(o) for o in offsets]
+    fetch = pltpu.make_async_copy(hidden_far, hidden, hidden_sem)
+    fetch.start()
     barrier = pltpu.get_barrier_semaphore()
     for other in greeted:
         pl.semaphore_signal(barrier, inc=1, device_id=other, device_id_type=MESH)
-    for h in range(2):
+    for h in range(2 * CHUNKS):
         whole[place, h, core] = weight[:, h * width : (h + 1) * width]
     pl.semaphore_wait(barrier, len(greeted))
 
@@ -140,9 +145,10 @@
     def landed(origin, h, c):
         piece(origin, h, c, to_sibling.at[origin, h], sibling).wait_recv()
 
-    send(place, side, to_ahead.at[place], ahead)
-    send(place, side, to_behind.at[place], behind)
-    for h in range(2):
+    for j in range(CHUNKS):
+        send(place, side * CHUNKS + j, to_ahead.at[place, j], ahead)
+        send(place, side * CHUNKS + j, to_behind.at[place, j], behind)
+    for h in range(2 * CHUNKS):
         send(place, h, to_sibling.at[place, h], sibling)
     kv_copies = []
     for o in offsets:
@@ -154,11 +160,11 @@
             device_id=near(o),
             device_id_type=MESH,
         )
-        copy.start()
         kv_copies.append(copy)
     own = pltpu.make_async_copy(picked.at[REACH], arrived.at[REACH], kv_own)
     own.start()
 
+    fetch.wait()
     tile = 32
     part = normed.shape[2]
 
@@ -171,41 +177,40 @@
         for chip in range(chips):
             normed[chip, rows, :] = scaled[:, chip * part : (chip + 1) * part]
 
-    columns = 256
-
     def multiply(origin, first):
-        for h in range(2):
+        for h in range(2 * CHUNKS):
             landed(origin, h, 1 - core)
 
-        @pl.loop(0, 2 * (width // columns))
-        def _(i):
-            h = lax.div(i, width // columns)
-            t = lax.rem(i, width // columns)
-            cols = pl.ds(pl.multiple_of(t * columns, columns), columns)
-            block = whole[origin, h, :, :, cols].reshape(2 * depth, columns)
+        @pl.loop(0, 2 * CHUNKS)
+        def _(h):
+            block = whole[origin, h].reshape(2 * depth, width)
             product = jnp.dot(normed[origin], block, preferred_element_type=jnp.float32)
             if first:
-                acc[h, :, cols] = product
+                acc[h] = product
             else:
-                acc[h, :, cols] += product
+                acc[h] += product
 
     def origins(k):
         return [chip_of(spot - turn * k)] + ([chip_of(spot + turn * k)] if k < half else [])
 
     def from_ring(k):
-        for origin, sem, other, last in zip(
-            origins(k), (to_ahead, to_behind), (ahead, behind), (half, half - 1)
-        ):
-            landed(origin, side, core)
-            if k < last:
-                send(origin, side, sem.at[origin], other)
-            send(origin, side, to_partner.at[origin], partner)
-            send(origin, side, to_sibling.at[origin, side], sibling)
+        for j in range(CHUNKS):
+            h = side * CHUNKS + j
+            for origin, sem, other, last in zip(
+                origins(k), (to_ahead, to_behind), (ahead, behind), (half, half - 1)
+            ):
+                landed(origin, h, core)
+                if k < last:
+                    send(origin, h, sem.at[origin, j], other)
+                send(origin, h, to_partner.at[origin, j], partner)
+                send(origin, h, to_sibling.at[origin, h], sibling)
 
     def from_partner(k):
-        for origin in origins(k):
-            landed(origin, 1 - side, core)
-            send(origin, 1 - side, to_sibling.at[origin, 1 - side], sibling)
+        for j in range(CHUNKS):
+            h = (1 - side) * CHUNKS + j
+            for origin in origins(k):
+                landed(origin, h, core)
+                send(origin, h, to_sibling.at[origin, h], sibling)
 
     def multiply_step(k):
         for origin in origins(k):
@@ -213,6 +218,9 @@
 
     multiply(place, True)
     for k in range(1, half + 4):
+        if k == KV_STEP:
+            for copy in kv_copies:
+                copy.start()
         if k <= half:
             from_ring(k)
         if 1 <= k - 2 <= half:
@@ -220,12 +228,9 @@
         if 1 <= k - 3 <= half:
             multiply_step(k - 3)
 
-    for h in range(2):
-        for t in range(width // columns):
-            lane = h * width + t * columns
-            query[:, lane : lane + columns] = (
-                acc[h, :, t * columns : (t + 1) * columns] + bias[:, lane : lane + columns]
-            ).astype(jnp.bfloat16)
+    for h in range(2 * CHUNKS):
+        lanes = slice(h * width, (h + 1) * width)
+        query[:, lanes] = (acc[h] + bias[:, lanes]).astype(jnp.bfloat16)
     for copy in sent:
         copy.wait_send()
     for copy in kv_copies:
@@ -247,23 +252,25 @@
             jax.ShapeDtypeStruct((rows, outputs), jnp.bfloat16),
             jax.ShapeDtypeStruct(picked.shape, picked.dtype),
         ),
-        in_specs=[vmem, vmem, vmem, vmem, anywhere],
+        in_specs=[anywhere, vmem, vmem, vmem, anywhere],
         out_specs=(vmem, anywhere),
         scratch_shapes=[
-            pltpu.VMEM((chips, 2, 2, depth, outputs // 2), jnp.bfloat16),
+            pltpu.VMEM((chips, 2 * CHUNKS, 2, depth, outputs // (2 * CHUNKS)), jnp.bfloat16),
             pltpu.VMEM((chips, rows, features // chips), jnp.bfloat16),
-            pltpu.VMEM((2, rows, outputs // 2), jnp.float32),
-            dma((chips, 2, 2)),
-            dma((chips,)),
-            dma((chips,)),
-            dma((chips, 2)),
-            dma((chips,)),
+            pltpu.VMEM((2 * CHUNKS, rows, outputs // (2 * CHUNKS)), jnp.float32),
+            dma((chips, 2 * CHUNKS, 2)),
+            dma((chips, CHUNKS)),
+            dma((chips, CHUNKS)),
+            dma((chips, 2 * CHUNKS)),
+            dma((chips, CHUNKS)),
             dma((span,)),
             dma((span,)),
             dma,
+            pltpu.VMEM((rows, features), jnp.bfloat16),
+            dma,
         ],
         compiler_params=pltpu.CompilerParams(
-            collective_id=1, has_side_effects=True, vmem_limit_bytes=56 * 1024 * 1024
+            collective_id=1, has_side_effects=True, vmem_limit_bytes=58 * 1024 * 1024
         ),
         cost_estimate=pl.CostEstimate(
             flops=2 * rows * features * outputs,
@@ -325,7 +332,7 @@
             out_specs=by_head,
         ),
         out_shape=jax.ShapeDtypeStruct(query.shape, jnp.bfloat16),
-        compiler_params=pltpu.CompilerParams(vmem_limit_bytes=40 * 1024 * 1024),
+        compiler_params=pltpu.CompilerParams(vmem_limit_bytes=58 * 1024 * 1024),
     )(slots.reshape(-1), hole, fill_len, query, arrived, arrived)
 
 

time: 237 us -> 192 us (0.81)
  Pallas kernels: 221 us -> 184 us
  local copies, waits for them, and re-layouts: 12.9 us -> 4.41 us
    pallas_call x1, Pallas kernels: 190 us -> 148 us  [projected(): pl.pallas_call(functools.partial(project_kernel, chips, lax.axis_size('gr...]
    unnamed x18 -> x8, local copies, waits for them, and re-layouts: 8.52 us -> 0.02 us
    pallas_call x1, Pallas kernels: 0.97 us -> 6.24 us  [picked_blocks(): pl.pallas_call(pick_kernel, grid_spec=pltpu.PrefetchScalarGridSpec(num_sc...]
where the time goes in v3:
time: 192 us; the launch traced here: 191 us
  Pallas kernels  184 us (96%)
  local copies, waits for them, and re-layouts  4.41 us (2%)
  other arithmetic  1.93 us (1%)
    pallas_call x1, Pallas kernels, projected(): pl.pallas_call(functools.partial(project_kernel, chips, lax.axis_size('gr...  148 us
    pallas_call x1, Pallas kernels, attend(): pl.pallas_call(attend_kernel, grid_spec=pltpu.PrefetchScalarGridSpec(num_...  20.6 us
    pallas_call x1, Pallas kernels, exchanged(): pl.pallas_call(exchange_kernel, out_shape=jax.ShapeDtypeStruct((span, 8,...  9.47 us
    pallas_call x1, Pallas kernels, picked_blocks(): pl.pallas_call(pick_kernel, grid_spec=pltpu.PrefetchScalarGridSpec(num_sc...  6.24 us

profile of v3, /device:TPU:0, one launch (start us, length us, event | category | flops | bytes accessed | tf_op | source)
XLA Modules:
  0.0 190.9 jit_solution(8718456740251931680)
XLA Ops:
  0.0 0.0 copy-start
  0.0 1.3 pad.4.ids_ref
  1.3 9.5 %shard_map.91 = s32[5,8,128]{2,1,0:T(8,128)} custom-call(s32[8,128]{1,0:T(8,128)} %pad.4.ids_ref), custom_call_target="tpu_custom_call" | custom-call | tf_op jit(solution)/shard_map/pallas_call | solution.py:53
  10.8 0.7 slice.7
  11.5 0.1 copy.12
  11.6 0.1 copy.13
  11.7 0.1 reshape.54
  11.8 0.0 copy-done
  11.8 0.7 gather_fusion.1
  12.5 0.1 reshape.53
  12.6 0.6 fusion.2.slots
  13.2 0.0 copy-start.1
  13.2 6.2 %shard_map.92.picked = bf16[5,2,512,512]{3,2,1,0:T(8,128)(2,1)} custom-call(s32[5]{0:T(128)} %fusion.2.slots, bf16[4,2,512,512]{3,2,1,0:T(8,128)(2,1)} %in_ref.1), custom_call_target="tpu_custom_call" | custom-call | tf_op jit(solution)/shard_map/pallas_call | solution.py:70
  19.5 0.0 copy-done.1
  19.5 0.6 reshape.42.bias
  20.1 148.1 %shard_map.93 = (bf16[384,2560]{1,0:T(8,128)(2,1)}, bf16[5,2,512,512]{3,2,1,0:T(8,128)(2,1)}) custom-call(bf16[384,5120]{1,0:T(8,128)(2,1)} %hidden_far.1, f32[1,5120]{1,0:T(1,128)} %bitcast.5, bf16[320,2560]{1,0:T(8,128)(2,1)} %weight.1, f32[1,2560]{1,0:T(1,128)} %reshape.42.bias, bf16[5,2,512,512]{3,2,1,0:T(8,128)(2,1)} %shard_map.92.picked), custom_call_target="tpu_custom_call" | custom-call | flops 10066329600 | bytes 14417920 | tf_op jit(solution)/shard_map/pallas_call | solution.py:249
  168.2 0.0 copy-done.2
  168.3 0.1 reshape.46
  168.3 0.6 gather_fusion
  169.0 0.6 and_select_fusion.slots
  169.5 0.1 multiply_reduce_fusion
  169.7 0.0 copy-done.3
  169.7 0.6 sub.21.hole
  170.2 20.6 %shard_map.94 = bf16[384,2560]{1,0:T(8,128)(2,1)} custom-call(s32[4]{0:T(128)} %and_select_fusion.slots, s32[2]{0:T(128)} %sub.21.hole, s32[2]{0:T(128)} %fill.1, bf16[384,2560]{1,0:T(8,128)(2,1)} %get-tuple-element.7.q_ref, bf16[5,2,512,512]{3,2,1,0:T(8,128)(2,1)} %get-tuple-element.8.first_ref.second_ref, ...), custom_call_target="tpu_custom_call" | custom-call | tf_op jit(solution)/shard_map/pallas_call | solution.py:326
  (6 shorter events, 0.0 us)
Async XLA Ops:
  0.0 11.8 %copy-start = (s32[64]{0:T(128)S(1)}, s32[64]{0:T(128)}, u32[]{:S(2)}) copy-start(s32[64]{0:T(128)} %param.14) | copy-start | bytes 772
  13.2 6.2 %copy-start.1 = (f32[2560]{0:T(1024)S(1)}, f32[2560]{0:T(1024)}, u32[]{:S(2)}) copy-start(f32[2560]{0:T(1024)} %param.12) | copy-start | bytes 30724
  20.1 148.2 %copy-start.2 = (s32[2,2]{1,0:T(2,128)S(1)}, s32[2,2]{1,0:T(2,128)}, u32[]{:S(2)}) copy-start(s32[2,2]{1,0:T(2,128)} %param.15) | copy-start | bytes 52
  20.1 149.6 %copy-start.3 = (s32[2]{0:T(128)S(1)}, s32[2]{0:T(128)}, u32[]{:S(2)}) copy-start(s32[2]{0:T(128)} %param.16) | copy-start | bytes 28

commit v4 on v3

--- a/solution.py
+++ b/solution.py
@@ -16,7 +16,7 @@
 REACH = 2
 MESH = pl.DeviceIdType.MESH
 CHUNKS = 2
-KV_STEP = 4
+KV_STEP = 3
 
 
 def exchange_kernel(ids_ref, out_ref, send_sem, recv_sem):
@@ -76,7 +76,7 @@
             out_specs=pl.BlockSpec(block, lambda i, slots: (i, 0, 0, 0)),
         ),
         out_shape=jax.ShapeDtypeStruct(slots.shape + kv_store.shape[1:], kv_store.dtype),
-        compiler_params=pltpu.CompilerParams(vmem_limit_bytes=58 * 1024 * 1024),
+        compiler_params=pltpu.CompilerParams(vmem_limit_bytes=16 * 1024 * 1024),
     )(slots, kv_store)
 
 
@@ -110,7 +110,7 @@
     behind = {"blk": chip_of(spot - turn) * 2 + core}
     sibling = {"blk": me + turn}
     partner = {"groups": group + 1 - 2 * side}
-    offsets = [o for o in (1, -1, 2, -2)]
+    offsets = [o for o in (2, -2, 1, -1)]
 
     def near(o):
         return {"blk": lax.rem(me + o + count, count)}
@@ -218,11 +218,11 @@
 
     multiply(place, True)
     for k in range(1, half + 4):
+        if k <= half:
+            from_ring(k)
         if k == KV_STEP:
             for copy in kv_copies:
                 copy.start()
-        if k <= half:
-            from_ring(k)
         if 1 <= k - 2 <= half:
             from_partner(k - 2)
         if 1 <= k - 3 <= half:

time: 192 us -> 190 us (0.990)
  Pallas kernels: 184 us -> 178 us
  local copies, waits for them, and re-layouts: 4.41 us -> 8.93 us
    pallas_call x1, Pallas kernels: 6.24 us -> 0.97 us  [picked_blocks(): pl.pallas_call(pick_kernel, grid_spec=pltpu.PrefetchScalarGridSpec(num_sc...]
    unnamed x8 -> x12, local copies, waits for them, and re-layouts: 0.02 us -> 4.54 us
where the time goes in v4:
time: 190 us; the launch traced here: 189 us
  Pallas kernels  178 us (94%)
  local copies, waits for them, and re-layouts  8.93 us (5%)
    pallas_call x1, Pallas kernels, projected(): pl.pallas_call(functools.partial(project_kernel, chips, lax.axis_size('gr...  147 us
    pallas_call x1, Pallas kernels, attend(): pl.pallas_call(attend_kernel, grid_spec=pltpu.PrefetchScalarGridSpec(num_...  20.6 us
    pallas_call x1, Pallas kernels, exchanged(): pl.pallas_call(exchange_kernel, out_shape=jax.ShapeDtypeStruct((span, 8,...  9.48 us
    unnamed x12, local copies, waits for them, and re-layouts  4.54 us

profile of v4, /device:TPU:0, one launch (start us, length us, event | category | flops | bytes accessed | tf_op | source)
XLA Modules:
  0.0 188.6 jit_solution(10519730109224838732)
XLA Ops:
  0.0 0.0 copy-start
  0.0 1.3 pad.4.ids_ref
  1.3 9.5 %shard_map.91 = s32[5,8,128]{2,1,0:T(8,128)} custom-call(s32[8,128]{1,0:T(8,128)} %pad.4.ids_ref), custom_call_target="tpu_custom_call" | custom-call | tf_op jit(solution)/shard_map/pallas_call | solution.py:53
  10.8 0.7 slice.7
  11.5 0.1 copy.12
  11.6 0.1 copy.13
  11.7 0.1 reshape.54
  11.8 0.7 gather_fusion.1
  12.5 0.1 reshape.53
  12.6 0.1 fusion.2.slots
  12.7 0.0 copy-start.2
  12.7 2.2 %copy-done.2 = bf16[4,2,512,512]{3,2,1,0:T(8,128)(2,1)S(1)} copy-done((bf16[4,2,512,512]{3,2,1,0:T(8,128)(2,1)S(1)}, bf16[4,2,512,512]{3,2,1,0:T(8,128)(2,1)}, u32[]{:S(2)}) %copy-start.2) | copy-done | bytes 4194328
  14.9 1.0 shard_map.92.picked
  15.9 0.0 copy-start.1
  15.9 2.3 %copy-done.1 = bf16[5,2,512,512]{3,2,1,0:T(8,128)(2,1)} copy-done((bf16[5,2,512,512]{3,2,1,0:T(8,128)(2,1)}, bf16[5,2,512,512]{3,2,1,0:T(8,128)(2,1)S(1)}, u32[]{:S(2)}) %copy-start.1) | copy-done | bytes 5242904
  18.2 0.0 copy-done.3
  18.2 0.6 reshape.42.bias
  18.8 147.2 %shard_map.93 = (bf16[384,2560]{1,0:T(8,128)(2,1)}, bf16[5,2,512,512]{3,2,1,0:T(8,128)(2,1)}) custom-call(bf16[384,5120]{1,0:T(8,128)(2,1)} %hidden_far.1, f32[1,5120]{1,0:T(1,128)} %bitcast.5, bf16[320,2560]{1,0:T(8,128)(2,1)} %weight.1, f32[1,2560]{1,0:T(1,128)} %reshape.42.bias, bf16[5,2,512,512]{3,2,1,0:T(8,128)(2,1)} %copy-done.1), custom_call_target="tpu_custom_call" | custom-call | flops 10066329600 | bytes 14417920 | tf_op jit(solution)/shard_map/pallas_call | solution.py:249
  166.0 0.1 reshape.46
  166.1 0.6 gather_fusion
  166.8 0.6 and_select_fusion.slots
  167.4 0.1 multiply_reduce_fusion
  167.5 0.5 sub.21.hole
  168.0 20.6 %shard_map.94 = bf16[384,2560]{1,0:T(8,128)(2,1)} custom-call(s32[4]{0:T(128)} %and_select_fusion.slots, s32[2]{0:T(128)} %sub.21.hole, s32[2]{0:T(128)} %fill.1, bf16[384,2560]{1,0:T(8,128)(2,1)} %get-tuple-element.7.q_ref, bf16[5,2,512,512]{3,2,1,0:T(8,128)(2,1)} %get-tuple-element.8.first_ref.second_ref, ...), custom_call_target="tpu_custom_call" | custom-call | tf_op jit(solution)/shard_map/pallas_call | solution.py:326
  (10 shorter events, 0.0 us)
Async XLA Ops:
  0.0 11.8 %copy-start = (s32[64]{0:T(128)S(1)}, s32[64]{0:T(128)}, u32[]{:S(2)}) copy-start(s32[64]{0:T(128)} %param.14) | copy-start | bytes 772
  12.7 2.2 %copy-start.2 = (bf16[4,2,512,512]{3,2,1,0:T(8,128)(2,1)S(1)}, bf16[4,2,512,512]{3,2,1,0:T(8,128)(2,1)}, u32[]{:S(2)}) copy-start(bf16[4,2,512,512]{3,2,1,0:T(8,128)(2,1)} %in_ref.1) | copy-start | bytes 12582916
  14.9 3.3 %copy-start.3 = (f32[2560]{0:T(1024)S(1)}, f32[2560]{0:T(1024)}, u32[]{:S(2)}) copy-start(f32[2560]{0:T(1024)} %param.12) | copy-start | bytes 30724
  15.9 2.3 %copy-start.1 = (bf16[5,2,512,512]{3,2,1,0:T(8,128)(2,1)}, bf16[5,2,512,512]{3,2,1,0:T(8,128)(2,1)S(1)}, u32[]{:S(2)}) copy-start(bf16[5,2,512,512]{3,2,1,0:T(8,128)(2,1)S(1)} %shard_map.92.picked) | copy-start | bytes 15728644
  18.8 147.2 %copy-start.4 = (s32[2,2]{1,0:T(2,128)S(1)}, s32[2,2]{1,0:T(2,128)}, u32[]{:S(2)}) copy-start(s32[2,2]{1,0:T(2,128)} %param.15) | copy-start | bytes 52
  18.8 148.7 %copy-start.5 = (s32[2]{0:T(128)S(1)}, s32[2]{0:T(128)}, u32[]{:S(2)}) copy-start(s32[2]{0:T(128)} %param.16) | copy-start | bytes 28
